TPU v7x, 256 devices: a whole 4x4x8 slice. The times are simulated.
256 devices in a mesh: seq: 16 (over y, z_hi, core), head: 16 (over x, z_lo).
Axes of the slice: x: 4, y: 4, z: 8 (z_hi: 2, z_lo: 4; z = z_hi * 4 + z_lo), core: 2. Of those that a mesh axis runs over, the one named last changes fastest.
Arguments:
- gen_ids: int32 [16, 16], replicated, may hold values from 0 to 8191
- embed_rows: bfloat16 [8192, 8192], P('head', 'seq'), may hold values from -6 to 6
- w_query: bfloat16 [8192, 8192], P('seq', 'head'), may hold values from -0.0625 to 0.0625
- w_key: bfloat16 [8192, 8192], P('seq', 'head'), may hold values from -0.0625 to 0.0625
- w_value: bfloat16 [8192, 8192], P('seq', 'head'), may hold values from -0.0625 to 0.0625
- w_out: bfloat16 [8192, 8192], P('head', 'seq'), may hold values from -0.0625 to 0.0625
- prompt_keys: bfloat16 [8192, 8192], P('seq', 'head'), may hold values from -420 to 420
- prompt_values: bfloat16 [8192, 8192], P('seq', 'head'), may hold values from -6 to 6
Outputs:
- attn_out: bfloat16 [256, 8192], P('seq', 'head')
All inputs are finite; a program needn't handle non-finite values.
Results may differ from a plain program's by a relative error of at most 0.034.
Values may be sent and summed in bfloat16 or wider, within the bound.
A program may use at most 128 MiB of HBM per device.

v0:
```python
import math

import jax
import jax.numpy as jnp
from jax import lax
from jax.sharding import PartitionSpec as P

HD = 128


def combined_all(part, axis, combine):
    gathered = jax.tree.map(lambda a: lax.all_gather(a, axis), part)

    def take(source):
        return jax.tree.map(lambda a: lax.dynamic_index_in_dim(a, source, 0, False), gathered)

    return lax.fori_loop(
        1, lax.axis_size(axis), lambda source, state: combine(state, take(source)), take(0)
    )


def rotate(vectors, positions):
    half_size = vectors.shape[-1] // 2
    frequency = 10000.0 ** (-jnp.arange(half_size, dtype=jnp.float32) / half_size)
    angles = positions.astype(jnp.float32)[:, None] * frequency[None, :]
    cosine = jnp.cos(angles)[:, None, :]
    sine_part = jnp.sin(angles)[:, None, :]
    former = vectors[..., :half_size]
    latter = vectors[..., half_size:]
    return jnp.concatenate(
        [former * cosine - latter * sine_part, former * sine_part + latter * cosine], axis=-1
    )


def joined(earlier, latter):
    peak = jnp.maximum(earlier[0], latter[0])
    left_factor = jnp.exp(earlier[0] - peak)
    right_factor = jnp.exp(latter[0] - peak)
    weight_sum = earlier[1] * left_factor + latter[1] * right_factor
    summed = earlier[2] * left_factor[..., None] + latter[2] * right_factor[..., None]
    return (peak, weight_sum, summed)


def score_block(queries, prompt_key, head_count, score_scale):
    key_heads = prompt_key.reshape(prompt_key.shape[0], head_count, -1)
    return (
        jnp.einsum("nhd,phd->nhp", queries, key_heads, preferred_element_type=jnp.float32)
        * score_scale
    )


def weigh_values(scores, peak, prompt_value, head_count):
    value_heads = prompt_value.reshape(prompt_value.shape[0], head_count, -1)
    weights = jnp.exp(scores - peak[..., None])
    weight_sum = jnp.sum(weights, axis=-1)
    summed = jnp.einsum(
        "nhp,phd->nhd",
        weights.astype(jnp.bfloat16),
        value_heads,
        preferred_element_type=jnp.float32,
    )
    return (weight_sum, summed)


def body(gen_ids, embed_rows, w_query, w_key, w_value, w_out, prompt_keys, prompt_values):
    cands_all, step_count = gen_ids.shape
    seq_count = lax.axis_size("seq")
    seq_index = lax.axis_index("seq")
    local_width = w_query.shape[1]
    head_count = local_width // HD
    own_tokens = cands_all * step_count // seq_count
    cand_count = own_tokens // step_count
    score_scale = 1.0 / math.sqrt(HD)
    vocab_local = embed_rows.shape[0]
    shifted_ids = gen_ids.reshape(-1) - lax.axis_index("head") * vocab_local
    selector = (shifted_ids[:, None] == jnp.arange(vocab_local, dtype=jnp.int32)[None, :]).astype(
        jnp.bfloat16
    )
    picked = jnp.dot(selector, embed_rows, preferred_element_type=jnp.float32)
    embedded = lax.psum(picked.astype(jnp.bfloat16), "head")
    stacked = jnp.concatenate([w_query, w_key, w_value], axis=1)
    projected = lax.psum_scatter(
        jnp.dot(embedded, stacked, preferred_element_type=jnp.float32),
        "seq",
        scatter_dimension=0,
        tiled=True,
    )
    positions = prompt_keys.shape[0] * seq_count + jnp.arange(step_count, dtype=jnp.int32)
    shaped = projected.reshape(cand_count, step_count, 3, head_count, HD)
    queries = rotate(shaped[:, :, 0], positions).astype(jnp.bfloat16)
    gen_keys = rotate(shaped[:, :, 1], positions).astype(jnp.bfloat16)
    gen_values = shaped[:, :, 2].astype(jnp.bfloat16)
    causal = jnp.arange(step_count)[None, :] <= jnp.arange(step_count)[:, None]
    own_scores = (
        jnp.einsum("cshd,cthd->csht", queries, gen_keys, preferred_element_type=jnp.float32)
        * score_scale
    )
    own_scores = jnp.where(causal[None, :, None, :], own_scores, -jnp.inf)
    own_peak = jnp.max(own_scores, axis=-1)
    own_weights = jnp.exp(own_scores - own_peak[..., None])
    own_sum = jnp.sum(own_weights, axis=-1)
    own_summed = jnp.einsum(
        "csht,cthd->cshd",
        own_weights.astype(jnp.bfloat16),
        gen_values,
        preferred_element_type=jnp.float32,
    )
    own_part = (
        own_peak.reshape(own_tokens, head_count),
        own_sum.reshape(own_tokens, head_count),
        own_summed.reshape(own_tokens, head_count, HD),
    )
    flat_queries = queries.reshape(own_tokens, head_count, HD)
    all_queries = lax.all_gather(flat_queries, "seq", axis=0, tiled=True)
    scores = score_block(all_queries, prompt_keys, head_count, score_scale)
    peak = jnp.max(scores, axis=-1)
    weight_sum, summed = weigh_values(scores, peak, prompt_values, head_count)
    merged = combined_all((peak, weight_sum, summed), "seq", joined)
    prompt_result = tuple(
        (
            lax.dynamic_slice_in_dim(member, seq_index * own_tokens, own_tokens, 0)
            for member in merged
        )
    )
    final_peak, final_sum, final_summed = joined(prompt_result, own_part)
    attended = (
        (final_summed / final_sum[..., None]).astype(jnp.bfloat16).reshape(own_tokens, local_width)
    )
    partials = jnp.dot(
        attended,
        lax.all_gather(w_out, "seq", axis=1, tiled=True),
        preferred_element_type=jnp.float32,
    )
    attn_out = lax.psum_scatter(
        partials.astype(jnp.bfloat16), "head", scatter_dimension=1, tiled=True
    )
    return attn_out


def solution(mesh):
    return jax.shard_map(
        body,
        mesh=mesh,
        in_specs=(
            P(),
            P("head", "seq"),
            P("seq", "head"),
            P("seq", "head"),
            P("seq", "head"),
            P("head", "seq"),
            P("seq", "head"),
            P("seq", "head"),
        ),
        out_specs=P("seq", "head"),
        check_vma=False,
    )
```

profile of v0, /device:TPU:64, one launch (start us, length us, event | category | flops | bytes accessed | tf_op | source)
XLA Modules:
  0.0 593.2 jit_solution(1400750699923680902)
XLA Ops:
  6.5 0.8 broadcast_subtract_fusion
  7.4 2.1 convolution_convert_fusion.1
  9.5 158.3 %all-reduce.2.cloned.1.call-done = bf16[256,512]{1,0:T(8,128)(2,1)} async-done(((bf16[256,512]{1,0:T(8,128)(2,1)}), bf16[256,512]{1,0:T(8,128)(2,1)}) %all-reduce.2.cloned.1.call-update) | async-done | bytes 262160 | tf_op jit(solution)/shard_map/psum | solution.py:80
  167.8 3.2 fusion.7
  171.2 85.7 %reduce-scatter.3.cloned.1.call-done = f32[16,1536]{1,0:T(8,128)} async-done(((f32[256,1536]{1,0:T(8,128)}), f32[16,1536]{1,0:T(8,128)}) %reduce-scatter.3.cloned.1.call-update) | async-done | bytes 98320 | tf_op jit(solution)/shard_map/reduce_scatter | solution.py:82
  256.9 0.9 reshape.165
  258.1 29.3 %all_gather.24 = bf16[256,4,128]{2,0,1:T(8,128)(2,1)S(1)} all-gather(bf16[16,4,128]{2,0,1:T(8,128)(2,1)S(1)} %pad_maximum_fusion), channel_id=1, replica_groups=mesh['seq'=16,'head'=16] {'seq'}, dimensions={0}, use_global_device_ids=true | all-gather | bytes 278528 | tf_op jit(solution)/shard_map/all_gather | solution.py:114
  287.9 1.4 convolution_bitcast_fusion
  289.4 0.5 all-gather.6.cloned.1.call-update
  290.0 0.6 fusion.6
  290.5 27.8 %all-gather.1 = f32[4096,4]{0,1:T(4,128)S(1)} all-gather(f32[256,4]{0,1:T(4,128)S(1)} %fusion.6), channel_id=3, replica_groups=mesh['seq'=16,'head'=16] {'seq'}, dimensions={0}, use_global_device_ids=true | all-gather | bytes 69632 | tf_op jit(solution)/shard_map/all_gather | solution.py:12
  318.3 35.4 %all-gather = f32[4096,4]{0,1:T(4,128)S(1)} all-gather(f32[256,4]{0,1:T(4,128)S(1)} %get-tuple-element.231), channel_id=2, replica_groups=mesh['seq'=16,'head'=16] {'seq'}, dimensions={0}, use_global_device_ids=true | all-gather | bytes 69632 | tf_op jit(solution)/shard_map/all_gather | solution.py:12
  354.0 39.8 %all-gather.8.cloned.1.call-done = f32[4096,4,128]{2,0,1:T(8,128)} async-done(((f32[256,4,128]{2,0,1:T(8,128)}), f32[4096,4,128]{2,0,1:T(8,128)}) %all-gather.8.cloned.1.call-update) | async-done | bytes 8388624 | tf_op jit(solution)/shard_map/all_gather | solution.py:12
  393.7 1.1 slice.40
  395.2 40.6 %while.19 = (s32[]{:T(128)}, f32[256,4]{0,1:T(4,128)S(1)}, f32[256,4]{0,1:T(4,128)S(1)}, f32[256,4,128]{2,1,0:T(4,128)S(1)}, f32[16,256,4]{1,2,0:T(4,128)S(1)}, ...) while((s32[]{:T(128)}, f32[256,4]{0,1:T(4,128)S(1)}, ...), condition=%wide.region_5.6_spmd, body=%wide.region_4.5_spmd.sunk | while | flops 399365 | bytes 2678935 | solution.py:17
  395.5 1.1 constant_dynamic-slice_fusion.2
  396.6 1.3 fusion.65
  398.2 1.1 constant_dynamic-slice_fusion.2
  399.3 1.3 fusion.65
  400.9 1.1 constant_dynamic-slice_fusion.2
  402.0 1.3 fusion.65
  403.6 1.1 constant_dynamic-slice_fusion.2
  404.7 1.3 fusion.65
  406.3 1.1 constant_dynamic-slice_fusion.2
  407.4 1.3 fusion.65
  409.0 1.1 constant_dynamic-slice_fusion.2
  410.1 1.3 fusion.65
  411.7 1.1 constant_dynamic-slice_fusion.2
  412.8 1.3 fusion.65
  414.4 1.1 constant_dynamic-slice_fusion.2
  415.5 1.3 fusion.65
  417.1 1.1 constant_dynamic-slice_fusion.2
  418.2 1.3 fusion.65
  419.8 1.1 constant_dynamic-slice_fusion.2
  420.9 1.3 fusion.65
  422.5 1.1 constant_dynamic-slice_fusion.2
  423.6 1.3 fusion.65
  425.3 1.1 constant_dynamic-slice_fusion.2
  426.3 1.3 fusion.65
  428.0 1.1 constant_dynamic-slice_fusion.2
  429.0 1.3 fusion.65
  430.7 1.1 constant_dynamic-slice_fusion.2
  431.7 1.3 fusion.65
  433.4 1.1 constant_dynamic-slice_fusion.2
  434.4 1.3 fusion.65
  436.1 68.3 %all-gather.6.cloned.1.call-done = bf16[512,8192]{1,0:T(8,128)(2,1)} async-done(((bf16[512,512]{1,0:T(8,128)(2,1)}), bf16[512,8192]{1,0:T(8,128)(2,1)}) %all-gather.6.cloned.1.call-update) | async-done | bytes 8388624 | tf_op jit(solution)/shard_map/all_gather | solution.py:131
  504.4 5.3 convolution_convert_fusion
  509.7 76.9 %reduce-scatter.5.cloned.1.call-done = bf16[16,512]{1,0:T(8,128)(2,1)} async-done(((bf16[16,8192]{1,0:T(8,128)(2,1)}), bf16[16,512]{1,0:T(8,128)(2,1)}) %reduce-scatter.5.cloned.1.call-update) | async-done | bytes 16400 | tf_op jit(solution)/shard_map/reduce_scatter | solution.py:134
  (77 shorter events, 6.6 us)
Async XLA Ops:
  6.5 280.9 %copy-start = (bf16[512,512]{1,0:T(8,128)(2,1)S(1)}, bf16[512,512]{1,0:T(8,128)(2,1)}, u32[]{:S(2)}) copy-start(bf16[512,512]{1,0:T(8,128)(2,1)} %param.16) | copy-start | bytes 1572868
  6.5 161.3 %all-reduce.2.cloned.1.call-start = ((), (), s32[]{:S(2)}) async-start(), calls=%async_computation.2 | async-start | bytes 524288 | tf_op jit(solution)/shard_map/psum | solution.py:80
  9.5 247.4 %reduce-scatter.3.cloned.1.call-start = ((), (), s32[]{:S(2)}) async-start(), calls=%async_computation.3 | async-start | bytes 1671168 | tf_op jit(solution)/shard_map/reduce_scatter | solution.py:82
  171.0 116.9 %copy-start.1 = (bf16[512,512]{1,0:T(8,128)(2,1)S(1)}, bf16[512,512]{1,0:T(8,128)(2,1)}, u32[]{:S(2)}) copy-start(bf16[512,512]{1,0:T(8,128)(2,1)} %param.17) | copy-start | bytes 1572868
  171.0 222.7 %all-gather.8.cloned.1.call-start = ((), (), s32[]{:S(2)}) async-start(), calls=%async_computation.6 | async-start | bytes 8912896 | tf_op jit(solution)/shard_map/all_gather | solution.py:12
  289.3 215.1 %all-gather.6.cloned.1.call-start = ((), (), s32[]{:S(2)}) async-start(), calls=%async_computation.4 | async-start | bytes 8912896 | tf_op jit(solution)/shard_map/all_gather | solution.py:131
  289.9 296.8 %reduce-scatter.5.cloned.1.call-start = ((), (), s32[]{:S(2)}) async-start(), calls=%async_computation.5 | async-start | bytes 278528 | tf_op jit(solution)/shard_map/reduce_scatter | solution.py:134
Sparse Core Ops, SparseCore 0:
  10.0 157.8 all-reduce.1
  172.6 84.3 reduce-scatter.2
  289.4 104.2 all-gather.7
  396.5 107.8 all-gather.5
  509.8 76.7 reduce-scatter.4
where the time goes:
time: 600 us; the launch traced here: 593 us
  waiting for transfers between devices  430 us (72%)
  blocking collectives  92.5 us (15%)
  local copies, waits for them, and re-layouts  22.9 us (4%)
  other arithmetic  21.2 us (4%)
  between operations  13.3 us (2%)
  matrix products  12.9 us (2%)
    psum x1, waiting for transfers between devices, body(): embedded = lax.psum(picked.astype(jnp.bfloat16), 'head')  158 us
    reduce_scatter x1, waiting for transfers between devices, body(): lax.psum_scatter(jnp.dot(embedded, stacked, preferred_element_type=jnp.fl...  85.7 us
    reduce_scatter x1, waiting for transfers between devices, body(): lax.psum_scatter(partials.astype(jnp.bfloat16), 'head', scatter_dimension...  76.9 us
    all_gather x1, waiting for transfers between devices, body(): lax.all_gather(w_out, 'seq', axis=1, tiled=True)  68.3 us
    all_gather x2, blocking collectives, combined_all(): gathered = jax.tree.map(lambda a: lax.all_gather(a, axis), part)  63.2 us
    all_gather x1, waiting for transfers between devices, combined_all(): gathered = jax.tree.map(lambda a: lax.all_gather(a, axis), part)  39.8 us
    all_gather x1, blocking collectives, body(): all_queries = lax.all_gather(flat_queries, 'seq', axis=0, tiled=True)  29.3 us
    add x15, other arithmetic, joined(): earlier[2] * left_factor[..., None] + latter[2] * right_factor[..., None]  19 us
  transfers between devices with their start and end apart: 5, of which 5 were waited for; matrix products, arithmetic and copies ran while one was open for 7% of the time, Pallas kernels for 0%

commit v1 on v0

v1 whole, which is shorter than its diff:
```python
import math

import jax
import jax.numpy as jnp
import numpy as np
from jax import lax
from jax.experimental import pallas as pl
from jax.experimental.pallas import tpu as pltpu
from jax.sharding import PartitionSpec as P

MESH = pl.DeviceIdType.MESH
HD = 128
N = 16
B = 16
F = 512
HEADS = F // HD
ST = 128
EXP_SCALE = math.log2(math.e) / math.sqrt(HD)
f32 = jnp.float32
bf16 = jnp.bfloat16


def rows_of(block):
    return pl.ds(pl.multiple_of(block * B, B), B)


def rounded(x):
    return x.astype(bf16).astype(f32)


def slot_sum(ref, columns=slice(None)):
    part = ref[:, columns].astype(f32)
    return jnp.sum(part.reshape(N, B, part.shape[-1]), axis=0)


def turned(x, table):
    heads = []
    for j in range(HEADS):
        part = x[:, j * HD : (j + 1) * HD]
        heads.append(part * table[:B] + pltpu.roll(part, HD // 2, 1) * table[B:])
    return jnp.concatenate(heads, axis=1)


def kernel(
    ids_hbm, e_hbm, wq_hbm, wk_hbm, wv_hbm, wo_hbm, k_hbm, v_hbm, tab_hbm, out_ref,
    ids, emb, wq, wk, wv, wo, keys, values, tab,
    pick, r_emb, x_all, q_part, r_q, q_all, kv_part, r_kv, o_part, r_o, att, out_part, r_out,
    load_sem, send_sem, recv_sem,
):
    s = lax.axis_index("seq")
    h = lax.axis_index("head")

    loads = [
        pltpu.make_async_copy(src, dst, load_sem.at[i])
        for i, (src, dst) in enumerate(
            [(ids_hbm, ids), (e_hbm, emb), (tab_hbm, tab), (wq_hbm, wq), (wk_hbm, wk), (wv_hbm, wv),
             (k_hbm, keys), (v_hbm, values), (wo_hbm, wo)]
        )
    ]
    for load in loads:
        load.start()

    barrier = pltpu.get_barrier_semaphore()

    def greet(d, carry):
        pl.semaphore_signal(barrier, inc=1, device_id=(s, lax.rem(h + d, N)), device_id_type=MESH)
        pl.semaphore_signal(barrier, inc=1, device_id=(lax.rem(s + d, N), h), device_id_type=MESH)
        return carry

    lax.fori_loop(1, N, greet, 0)

    def along_head(j):
        return (s, j)

    def along_seq(j):
        return (j, h)

    def scatter(i, src, dst, me, place):
        def step(d, carry):
            j = lax.rem(me + d, N)
            pltpu.make_async_remote_copy(
                src_ref=src.at[rows_of(j)], dst_ref=dst.at[rows_of(me)],
                send_sem=send_sem.at[i], recv_sem=recv_sem.at[i],
                device_id=place(j), device_id_type=MESH,
            ).start()
            return carry

        lax.fori_loop(1, N, step, 0)
        dst[rows_of(me), :] = src[rows_of(me), :]

    def spread(i, ref, me, place):
        def step(d, carry):
            pltpu.make_async_remote_copy(
                src_ref=ref.at[rows_of(me)], dst_ref=ref.at[rows_of(me)],
                send_sem=send_sem.at[i], recv_sem=recv_sem.at[i],
                device_id=place(lax.rem(me + d, N)), device_id_type=MESH,
            ).start()
            return carry

        lax.fori_loop(1, N, step, 0)

    def all_of(i, ref, place, count=N - 1):
        part = ref.at[pl.ds(0, count * B)]
        return pltpu.make_async_remote_copy(
            src_ref=part, dst_ref=part, send_sem=send_sem.at[i], recv_sem=recv_sem.at[i],
            device_id=place, device_id_type=MESH,
        )

    head_peer = (s, lax.rem(h + 1, N))
    seq_peer = (lax.rem(s + 1, N), h)

    loads[0].wait()
    shifted = (ids[...] - h * F).astype(f32)
    eye = lax.broadcasted_iota(jnp.int32, (B, B), 0) == lax.broadcasted_iota(jnp.int32, (B, B), 1)
    entry = lax.broadcasted_iota(jnp.int32, (B, F), 1).astype(f32)
    chosen = []
    for c in range(N):
        row = jnp.broadcast_to(shifted[c : c + 1, :], (B, B))
        column = jnp.sum(jnp.where(eye, row, 0.0), axis=1, keepdims=True)
        chosen.append(jnp.where(column == entry, 1.0, 0.0).astype(bf16))
    selector = jnp.concatenate(chosen, axis=0)
    loads[1].wait()
    pick[...] = jnp.dot(selector, emb[...], preferred_element_type=f32).astype(bf16)

    pl.semaphore_wait(barrier, 2 * (N - 1))

    scatter(0, pick, r_emb, h, along_head)
    all_of(0, r_emb, head_peer).wait_recv()
    x_all[rows_of(h), :] = slot_sum(r_emb).astype(bf16)
    spread(1, x_all, h, along_head)
    loads[3].wait()
    all_of(1, x_all, head_peer).wait_recv()

    q_part[...] = jnp.dot(x_all[...], wq[...], preferred_element_type=f32).astype(bf16)
    scatter(2, q_part, r_q, s, along_seq)
    loads[4].wait()
    loads[5].wait()
    kv_part[:, :F] = jnp.dot(x_all[...], wk[...], preferred_element_type=f32).astype(bf16)
    kv_part[:, F:] = jnp.dot(x_all[...], wv[...], preferred_element_type=f32).astype(bf16)
    loads[2].wait()
    table = tab[...]
    all_of(2, r_q, seq_peer).wait_recv()
    queries = turned(slot_sum(r_q), table).astype(bf16)
    q_all[rows_of(s), :] = queries
    spread(3, q_all, s, along_seq)
    scatter(4, kv_part, r_kv, s, along_seq)
    loads[6].wait()
    loads[7].wait()
    all_of(3, q_all, seq_peer).wait_recv()

    lane = lax.broadcasted_iota(jnp.int32, (N * B, ST), 1)
    peaks = jnp.zeros((N * B, ST), f32)
    sums = jnp.zeros((N * B, ST), f32)
    for j in range(HEADS):
        cols = slice(j * HD, (j + 1) * HD)
        scores = lax.dot_general(
            q_all[:, cols], keys[:, cols], (((1,), (1,)), ((), ())), preferred_element_type=f32
        )
        peak = jnp.max(scores, axis=1, keepdims=True)
        weights = jnp.exp2((scores - peak) * EXP_SCALE)
        total = jnp.sum(weights, axis=1, keepdims=True)
        o_part[:, cols] = jnp.dot(
            weights.astype(bf16), values[:, cols], preferred_element_type=f32
        ).astype(bf16)
        peaks = jnp.where(lane == j, peak, peaks)
        sums = jnp.where(lane == j, total, sums)
    high = rounded(peaks)
    middle = rounded(peaks - high)
    low = rounded(peaks - high - middle)
    sum_high = rounded(sums)
    sum_low = rounded(sums - sum_high)
    packed = (
        high + pltpu.roll(middle, HEADS, 1) + pltpu.roll(low, 2 * HEADS, 1)
        + pltpu.roll(sum_high, 3 * HEADS, 1) + pltpu.roll(sum_low, 4 * HEADS, 1)
    )
    o_part[:, F:] = packed.astype(bf16)
    scatter(5, o_part, r_o, s, along_seq)

    all_of(4, r_kv, seq_peer).wait_recv()
    own_keys = turned(slot_sum(r_kv, slice(0, F)), table).astype(bf16)
    own_values = slot_sum(r_kv, slice(F, 2 * F)).astype(bf16)
    causal = lax.broadcasted_iota(jnp.int32, (B, B), 1) <= lax.broadcasted_iota(jnp.int32, (B, B), 0)
    own_lane = lax.broadcasted_iota(jnp.int32, (B, ST), 1)
    own_peaks = jnp.zeros((B, ST), f32)
    own_sums = jnp.zeros((B, ST), f32)
    own_out = []
    for j in range(HEADS):
        cols = slice(j * HD, (j + 1) * HD)
        scores = lax.dot_general(
            queries[:, cols], own_keys[:, cols], (((1,), (1,)), ((), ())), preferred_element_type=f32
        )
        scores = jnp.where(causal, scores, -jnp.inf)
        peak = jnp.max(scores, axis=1, keepdims=True)
        weights = jnp.exp2((scores - peak) * EXP_SCALE)
        total = jnp.sum(weights, axis=1, keepdims=True)
        own_out.append(jnp.dot(weights.astype(bf16), own_values[:, cols], preferred_element_type=f32))
        own_peaks = jnp.where(own_lane == j, peak, own_peaks)
        own_sums = jnp.where(own_lane == j, total, own_sums)

    all_of(5, r_o, seq_peer).wait_recv()
    stats = r_o[:, F:].astype(f32)
    part_peaks = stats + pltpu.roll(stats, ST - HEADS, 1) + pltpu.roll(stats, ST - 2 * HEADS, 1)
    part_sums = pltpu.roll(stats, ST - 3 * HEADS, 1) + pltpu.roll(stats, ST - 4 * HEADS, 1)
    part_peaks = part_peaks.reshape(N, B, ST)
    part_sums = part_sums.reshape(N, B, ST)
    top = jnp.maximum(jnp.max(part_peaks, axis=0), own_peaks)
    factor = jnp.exp2((part_peaks - top[None]) * EXP_SCALE)
    own_factor = jnp.exp2((own_peaks - top) * EXP_SCALE)
    weight_sum = jnp.sum(factor * part_sums, axis=0) + own_factor * own_sums
    for j in range(HEADS):
        cols = slice(j * HD, (j + 1) * HD)
        part = r_o[:, cols].astype(f32).reshape(N, B, HD)
        summed = jnp.sum(part * factor[:, :, j : j + 1], axis=0) + own_out[j] * own_factor[:, j : j + 1]
        att[rows_of(s), cols] = (summed / weight_sum[:, j : j + 1]).astype(bf16)
    spread(6, att, s, along_seq)
    loads[8].wait()
    all_of(6, att, seq_peer).wait_recv()

    out_part[...] = jnp.dot(att[...], wo[...], preferred_element_type=f32).astype(bf16)

    def send_out(d, carry):
        t = lax.rem(s + d, N)

        @pl.when((d > 0) | (s != h))
        def _():
            pltpu.make_async_remote_copy(
                src_ref=out_part.at[rows_of(t)], dst_ref=r_out.at[rows_of(h)],
                send_sem=send_sem.at[7], recv_sem=recv_sem.at[7],
                device_id=(t, s), device_id_type=MESH,
            ).start()

        return carry

    lax.fori_loop(0, N, send_out, 0)

    @pl.when(s == h)
    def _():
        r_out[rows_of(h), :] = out_part[rows_of(h), :]
        all_of(7, r_out, seq_peer, N - 1).wait_recv()

    @pl.when(s != h)
    def _():
        all_of(7, r_out, seq_peer, N).wait_recv()

    out_ref[...] = slot_sum(r_out).astype(bf16)

    for i, ref in enumerate((pick, x_all, q_part, q_all, kv_part, o_part, att)):
        all_of(i, ref, seq_peer).wait_send()

    @pl.when(s == h)
    def _():
        all_of(7, out_part, seq_peer, N - 1).wait_send()

    @pl.when(s != h)
    def _():
        all_of(7, out_part, seq_peer, N).wait_send()


def rotation_table(first, count):
    half = HD // 2
    frequency = 10000.0 ** (-np.arange(half, dtype=np.float64) / half)
    angles = (first + np.arange(count, dtype=np.float64))[:, None] * frequency[None, :]
    cosine, sine = np.cos(angles), np.sin(angles)
    return np.concatenate(
        [np.concatenate([cosine, cosine], 1), np.concatenate([-sine, sine], 1)], 0
    ).astype(np.float32)


def body(gen_ids, embed_rows, w_query, w_key, w_value, w_out, prompt_keys, prompt_values):
    table = jnp.asarray(rotation_table(prompt_keys.shape[0] * N, B))
    tokens = N * B
    wide = lambda width: pltpu.VMEM((tokens, width), bf16)
    block = pltpu.VMEM((F, F), bf16)
    return pl.pallas_call(
        kernel,
        out_shape=jax.ShapeDtypeStruct((B, F), bf16),
        in_specs=[pl.BlockSpec(memory_space=pl.ANY)] * 9,
        out_specs=pl.BlockSpec(memory_space=pltpu.VMEM),
        scratch_shapes=[
            pltpu.VMEM((N, B), jnp.int32), block, block, block, block, block, block, block,
            pltpu.VMEM((2 * B, HD), f32),
            wide(F), wide(F), wide(F), wide(F), wide(F), wide(F), wide(2 * F), wide(2 * F),
            wide(F + ST), wide(F + ST), wide(F), wide(F), wide(F),
            pltpu.SemaphoreType.DMA((9,)),
            pltpu.SemaphoreType.DMA((8,)),
            pltpu.SemaphoreType.DMA((8,)),
        ],
        compiler_params=pltpu.CompilerParams(
            collective_id=0, has_side_effects=True, vmem_limit_bytes=62 * 1024 * 1024
        ),
    )(gen_ids, embed_rows, w_query, w_key, w_value, w_out, prompt_keys, prompt_values, table)


def solution(mesh):
    return jax.shard_map(
        body,
        mesh=mesh,
        in_specs=(
            P(), P("head", "seq"), P("seq", "head"), P("seq", "head"), P("seq", "head"),
            P("head", "seq"), P("seq", "head"), P("seq", "head"),
        ),
        out_specs=P("seq", "head"),
        check_vma=False,
    )
```

time: 600 us -> 94.7 us (0.16)
  the two profiles are of different devices: /device:TPU:64 before, /device:TPU:25 now
where the time goes in v1:
time: 94.7 us; the launch traced here: 94.5 us
  Pallas kernels  93.1 us (98%)
  local copies, waits for them, and re-layouts  1.32 us (1%)
    pallas_call x1, Pallas kernels, body(): pl.pallas_call(kernel, out_shape=jax.ShapeDtypeStruct((B, F), bf16), in_s...  93.1 us

profile of v1, /device:TPU:25, one launch (start us, length us, event | category | flops | bytes accessed | tf_op | source)
XLA Modules:
  0.0 94.5 jit_solution(6178246459532649469)
XLA Ops:
  0.0 93.1 %shard_map.91 = bf16[16,512]{1,0:T(8,128)(2,1)} custom-call(s32[16,16]{1,0:T(8,128)} %ids_hbm.1, bf16[512,512]{1,0:T(8,128)(2,1)} %e_hbm.1, bf16[512,512]{1,0:T(8,128)(2,1)} %wq_hbm.1, bf16[512,512]{1,0:T(8,128)(2,1)} %wk_hbm.1, bf16[512,512]{1,0:T(8,128)(2,1)} %wv_hbm.1, bf16[512,512]{1,0:T(8,128)(2,1)} %wo_hbm.1, bf16[512,512]{1,0:T(8,128)(2,1)} %k_hbm.1, ...), custom_call_target="tpu_custom_call" | custom-call | tf_op jit(solution)/shard_map/pallas_call | solution.py:274
  93.1 1.3 %copy.11 = bf16[16,512]{1,0:T(8,128)(2,1)} copy(bf16[16,512]{1,0:T(8,128)(2,1)} %shard_map.91) | data formatting | bytes 32768

commit v2 on v1

v2 whole, which is shorter than its diff:
```python
import math

import jax
import jax.numpy as jnp
import numpy as np
from jax import lax
from jax.experimental import pallas as pl
from jax.experimental.pallas import tpu as pltpu
from jax.sharding import PartitionSpec as P

MESH = pl.DeviceIdType.MESH
HD = 128
N = 16
B = 16
F = 512
HALF = N * B // 2
YS = 4
PROMPT = 8 * F
CHUNK = 1024
EXP_SCALE = math.log2(math.e) / math.sqrt(HD)
f32 = jnp.float32
bf16 = jnp.bfloat16
EMB_RS, EMB_AG, Q_RS, Q_Z, K_MOVE, V_MOVE, K_PAIR, V_PAIR, KV_RS, KV_Z, O_Z, W_MOVE, W_TURN, ATT_AG, OUT_RS = range(15)


def part(index, size):
    return pl.ds(pl.multiple_of(index * size, size), size)


def rounded(x):
    return x.astype(bf16).astype(f32)


def slot_sum(ref, slots, rows):
    return jnp.sum(ref[...].astype(f32).reshape(slots, rows, ref.shape[-1]), axis=0)


def turned(x, cosine, sine):
    return x * cosine + pltpu.roll(x, HD // 2, 1) * sine


def kernel(
    ids_hbm, e_hbm, wq_hbm, wk_hbm, wv_hbm, wo_hbm, k_hbm, v_hbm, tab_hbm, out_ref,
    ids, emb, wq, wk, wv, tab, keys, values, w_stage, w_all,
    pick, r_emb, x_all, q_part, r_q, q_mine, q_other, kv_part, r_kv, kv_mine, kv_other,
    scores, o_mine, o_other, att, att_all, out_part, r_out,
    load_sem, send_sem, recv_sem,
):
    s = lax.axis_index("seq")
    h = lax.axis_index("head")
    y, zh, c = s // 4, lax.rem(s // 2, 2), lax.rem(s, 2)
    x, zl = h // 4, lax.rem(h, 4)
    sibling = (s + 1 - 2 * c, h)
    antipode = (s + 2 - 4 * zh, h)
    pos = y * 2 + c
    own = lax.rem(s, 4)
    out_self = own == zl

    loads = [
        pltpu.make_async_copy(src, dst, load_sem.at[i])
        for i, (src, dst) in enumerate(
            [
                (ids_hbm, ids), (e_hbm, emb), (wq_hbm, wq), (wk_hbm, wk), (wv_hbm, wv), (tab_hbm, tab),
                (k_hbm.at[:, part(y, HD)], keys.at[part(c * YS + y, F)]),
                (v_hbm.at[:, part(y, HD)], values.at[part(c * YS + y, F)]),
                (wo_hbm.at[part(y, HD)], w_stage.at[part(y, HD)]),
            ]
        )
    ]
    for load in loads:
        load.start()

    barrier = pltpu.get_barrier_semaphore()

    def greet(device):
        pl.semaphore_signal(barrier, inc=1, device_id=device, device_id_type=MESH)

    def in_group(e):
        return ((e // 2) * 4 + zh * 2 + lax.rem(e, 2), h)

    def greet_plane(d, carry):
        greet((s, lax.rem(h + d, N)))
        return carry

    def greet_group(d, carry):
        greet(in_group(lax.rem(pos + d, 8)))
        return carry

    lax.fori_loop(1, N, greet_plane, 0)
    greet(antipode)
    lax.fori_loop(1, 8, greet_group, 0)

    def copy(i, src, dst, device):
        return pltpu.make_async_remote_copy(
            src_ref=src, dst_ref=dst, send_sem=send_sem.at[i], recv_sem=recv_sem.at[i],
            device_id=device, device_id_type=MESH,
        )

    def rows(i, ref, count):
        return copy(i, ref.at[pl.ds(0, count)], ref.at[pl.ds(0, count)], sibling)

    loads[0].wait()
    shifted = (ids[...] - h * F).astype(f32)
    eye = lax.broadcasted_iota(jnp.int32, (B, B), 0) == lax.broadcasted_iota(jnp.int32, (B, B), 1)
    entry = lax.broadcasted_iota(jnp.int32, (B, F), 1).astype(f32)
    chosen = []
    for b in range(N):
        t = (b % 8) * 2 + b // 8
        row = jnp.broadcast_to(shifted[t : t + 1, :], (B, B))
        column = jnp.sum(jnp.where(eye, row, 0.0), axis=1, keepdims=True)
        chosen.append(jnp.where(column == entry, 1.0, 0.0).astype(bf16))
    selector = jnp.concatenate(chosen, axis=0)
    loads[1].wait()
    pick[...] = jnp.dot(selector, emb[...], preferred_element_type=f32).astype(bf16)

    pl.semaphore_wait(barrier, 15 + 7 + 1)

    def send_pick(d, carry):
        j = lax.rem(h + d, N)
        copy(EMB_RS, pick.at[part(j, B)], r_emb.at[part(h, B)], (s, j)).start()
        return carry

    lax.fori_loop(1, N, send_pick, 0)
    r_emb[part(h, B), :] = pick[part(h, B), :]

    def move_prompt(d, carry):
        j = lax.rem(y + d, YS)
        device = (j * 4 + zh * 2 + c, h)
        slot = part(c * YS + y, F)
        copy(K_MOVE, k_hbm.at[:, part(j, HD)], keys.at[slot], device).start()
        copy(V_MOVE, v_hbm.at[:, part(j, HD)], values.at[slot], device).start()
        copy(W_MOVE, wo_hbm.at[part(j, HD)], w_stage.at[part(y, HD)], device).start()
        return carry

    lax.fori_loop(1, YS, move_prompt, 0)

    rows(EMB_RS, r_emb, 15 * B).wait_recv()
    x_all[part(h, B), :] = slot_sum(r_emb, N, B).astype(bf16)

    def send_x(d, carry):
        copy(EMB_AG, x_all.at[part(h, B)], x_all.at[part(h, B)], (s, lax.rem(h + d, N))).start()
        return carry

    lax.fori_loop(1, N, send_x, 0)
    loads[2].wait()
    rows(EMB_AG, x_all, 15 * B).wait_recv()

    projected = jnp.dot(x_all[...], wq[...], preferred_element_type=f32).astype(bf16)
    for j in range(YS):
        q_part[j * 2 * HALF : (j + 1) * 2 * HALF, :] = projected[:, j * HD : (j + 1) * HD]

    def send_q(d, carry):
        e = lax.rem(pos + d, 8)
        copy(Q_RS, q_part.at[part(e, HALF)], r_q.at[part(pos, HALF)], in_group(e)).start()
        return carry

    lax.fori_loop(1, 8, send_q, 0)
    r_q[part(pos, HALF), :] = q_part[part(pos, HALF), :]

    loads[3].wait()
    loads[4].wait()
    for i, w in enumerate((wk, wv)):
        projected = jnp.dot(x_all[...], w[...], preferred_element_type=f32).astype(bf16)
        for j in range(YS):
            for e in range(2):
                first = ((j * 2 + e) * 2 + i) * HALF
                kv_part[first : first + HALF, :] = projected[e * HALF : (e + 1) * HALF, j * HD : (j + 1) * HD]

    def send_kv(d, carry):
        e = lax.rem(pos + d, 8)
        copy(KV_RS, kv_part.at[part(e, 2 * HALF)], r_kv.at[part(pos, 2 * HALF)], in_group(e)).start()
        return carry

    lax.fori_loop(1, 8, send_kv, 0)
    r_kv[part(pos, 2 * HALF), :] = kv_part[part(pos, 2 * HALF), :]

    loads[8].wait()
    rows(W_MOVE, w_stage, 3 * HD).wait_recv()

    def turn_w(d, carry):
        i = lax.rem(x + d, 4)
        copy(W_TURN, w_stage.at[part(i, HD)], w_all.at[part(x, HD)], (s, 4 * i + zl)).start()
        return carry

    lax.fori_loop(1, 4, turn_w, 0)
    w_all[part(x, HD), :] = w_stage[part(x, HD), :]

    loads[6].wait()
    loads[7].wait()
    rows(K_MOVE, keys, 3 * F).wait_recv()
    rows(V_MOVE, values, 3 * F).wait_recv()
    pair_rows = part(c, PROMPT // 2)
    copy(K_PAIR, keys.at[pair_rows], keys.at[pair_rows], sibling).start()
    copy(V_PAIR, values.at[pair_rows], values.at[pair_rows], sibling).start()

    rows(Q_RS, r_q, 7 * HALF).wait_recv()
    q_sum = slot_sum(r_q, 8, HALF)
    q_mine[...] = q_sum.astype(bf16)
    copy(Q_Z, q_mine, q_other, antipode).start()

    rows(KV_RS, r_kv, 14 * HALF).wait_recv()
    kv_sum = slot_sum(r_kv, 8, 2 * HALF)

    kv_mine[...] = kv_sum.astype(bf16)
    copy(KV_Z, kv_mine, kv_other, antipode).start()

    loads[5].wait()
    cosine = jnp.concatenate([tab[:B, :]] * 8, axis=0)
    sine = jnp.concatenate([tab[B:, :]] * 8, axis=0)
    rows(Q_Z, q_other, HALF).wait_recv()
    queries = turned(q_sum + q_other[...].astype(f32), cosine, sine).astype(bf16)

    rows(K_PAIR, keys, PROMPT // 2).wait_recv()
    peak = None
    for i in range(PROMPT // CHUNK):
        block = lax.dot_general(
            queries, keys[i * CHUNK : (i + 1) * CHUNK, :], (((1,), (1,)), ((), ())), preferred_element_type=f32
        )
        scores[:, i * CHUNK : (i + 1) * CHUNK] = block
        top = jnp.max(block, axis=1, keepdims=True)
        peak = top if peak is None else jnp.maximum(peak, top)
    rows(V_PAIR, values, PROMPT // 2).wait_recv()
    weight_sum = jnp.zeros((HALF, 1), f32)
    summed = jnp.zeros((HALF, HD), f32)
    for i in range(PROMPT // CHUNK):
        weights = jnp.exp2((scores[:, i * CHUNK : (i + 1) * CHUNK] - peak) * EXP_SCALE)
        weight_sum += jnp.sum(weights, axis=1, keepdims=True)
        summed += jnp.dot(
            weights.astype(bf16), values[i * CHUNK : (i + 1) * CHUNK, :], preferred_element_type=f32
        )

    lane = lax.broadcasted_iota(jnp.int32, (HALF, HD), 1)
    high = rounded(peak)
    middle = rounded(peak - high)
    sum_high = rounded(weight_sum)
    packed = jnp.zeros((HALF, HD), f32)
    for i, stat in enumerate(
        (high, middle, rounded(peak - high - middle), sum_high, rounded(weight_sum - sum_high))
    ):
        packed = jnp.where(lane == i, stat, packed)
    o_mine[:HALF, :] = summed.astype(bf16)
    o_mine[HALF:, :] = packed.T[:B, :].astype(bf16)
    copy(O_Z, o_mine, o_other, antipode).start()

    rows(KV_Z, kv_other, 2 * HALF).wait_recv()
    both = kv_sum + kv_other[...].astype(f32)
    own_keys = turned(both[:HALF], cosine, sine).astype(bf16)
    own_values = both[HALF:].astype(bf16)
    own_scores = lax.dot_general(queries, own_keys, (((1,), (1,)), ((), ())), preferred_element_type=f32)
    token = lax.broadcasted_iota(jnp.int32, (HALF, HALF), 0)
    other = lax.broadcasted_iota(jnp.int32, (HALF, HALF), 1)
    seen = (token // B == other // B) & (other <= token)
    own_scores = jnp.where(seen, own_scores, -jnp.inf)
    own_peak = jnp.max(own_scores, axis=1, keepdims=True)
    own_weights = jnp.exp2((own_scores - own_peak) * EXP_SCALE)
    own_sum = jnp.sum(own_weights, axis=1, keepdims=True)
    own_out = jnp.dot(own_weights.astype(bf16), own_values, preferred_element_type=f32)

    rows(O_Z, o_other, HALF + B).wait_recv()
    stats = o_other[HALF:, :].astype(f32).T
    far_peak = stats[:, 0:1] + stats[:, 1:2] + stats[:, 2:3]
    far_sum = stats[:, 3:4] + stats[:, 4:5]
    top = jnp.maximum(jnp.maximum(peak, own_peak), far_peak)
    near = jnp.exp2((peak - top) * EXP_SCALE)
    far = jnp.exp2((far_peak - top) * EXP_SCALE)
    mine = jnp.exp2((own_peak - top) * EXP_SCALE)
    total = near * weight_sum + far * far_sum + mine * own_sum
    joined = near * summed + far * o_other[:HALF, :].astype(f32) + mine * own_out
    att[...] = (joined / total).astype(bf16)

    place = x * 2 + c

    def send_att(d, carry):
        e = lax.rem(place + d, 8)
        device = (s - c + lax.rem(e, 2), (e // 2) * 4 + zl)
        copy(ATT_AG, att, att_all.at[part(place, HALF)], device).start()
        return carry

    lax.fori_loop(1, 8, send_att, 0)
    att_all[part(place, HALF), :] = att[...]
    rows(W_TURN, w_all, 3 * HD).wait_recv()
    rows(ATT_AG, att_all, 7 * HALF).wait_recv()

    attended = jnp.concatenate(
        [
            jnp.concatenate([att_all[(i * 2 + e) * HALF : (i * 2 + e + 1) * HALF, :] for i in range(4)], axis=1)
            for e in range(2)
        ],
        axis=0,
    )
    out_part[...] = jnp.dot(attended, w_all[...], preferred_element_type=f32).astype(bf16)
    out_slot = part(y * 4 + zl, B)

    def send_out(d, carry):
        t = lax.rem(s + d, N)
        block = lax.rem(t, 2) * 8 + t // 2

        @pl.when((d > 0) | jnp.logical_not(out_self))
        def _():
            copy(OUT_RS, out_part.at[part(block, B)], r_out.at[out_slot], (t, 4 * x + own)).start()

        return carry

    lax.fori_loop(0, N, send_out, 0)

    @pl.when(out_self)
    def _():
        r_out[out_slot, :] = out_part[part(c * 8 + s // 2, B), :]
        rows(OUT_RS, r_out, 15 * B).wait_recv()

    @pl.when(jnp.logical_not(out_self))
    def _():
        rows(OUT_RS, r_out, 16 * B).wait_recv()

    out_ref[...] = slot_sum(r_out, N, B).astype(bf16)

    rows(EMB_RS, pick, 15 * B).wait_send()
    rows(EMB_AG, x_all, 15 * B).wait_send()
    rows(K_MOVE, keys, 3 * F).wait_send()
    rows(V_MOVE, values, 3 * F).wait_send()
    rows(W_MOVE, w_stage, 3 * HD).wait_send()
    rows(K_PAIR, keys, PROMPT // 2).wait_send()
    rows(V_PAIR, values, PROMPT // 2).wait_send()
    rows(Q_RS, q_part, 7 * HALF).wait_send()
    rows(Q_Z, q_mine, HALF).wait_send()
    rows(KV_RS, kv_part, 14 * HALF).wait_send()
    rows(KV_Z, kv_mine, 2 * HALF).wait_send()
    rows(O_Z, o_mine, HALF + B).wait_send()
    rows(W_TURN, w_stage, 3 * HD).wait_send()
    rows(ATT_AG, att_all, 7 * HALF).wait_send()

    @pl.when(out_self)
    def _():
        rows(OUT_RS, out_part, 15 * B).wait_send()

    @pl.when(jnp.logical_not(out_self))
    def _():
        rows(OUT_RS, out_part, 16 * B).wait_send()


def rotation_table(first, count):
    half = HD // 2
    frequency = 10000.0 ** (-np.arange(half, dtype=np.float64) / half)
    angles = (first + np.arange(count, dtype=np.float64))[:, None] * frequency[None, :]
    cosine, sine = np.cos(angles), np.sin(angles)
    return np.concatenate(
        [np.concatenate([cosine, cosine], 1), np.concatenate([-sine, sine], 1)], 0
    ).astype(np.float32)


def body(gen_ids, embed_rows, w_query, w_key, w_value, w_out, prompt_keys, prompt_values):
    table = jnp.asarray(rotation_table(prompt_keys.shape[0] * N, B))

    def held(count, width=HD, dtype=bf16):
        return pltpu.VMEM((count, width), dtype)

    return pl.pallas_call(
        kernel,
        out_shape=jax.ShapeDtypeStruct((B, F), bf16),
        in_specs=[pl.BlockSpec(memory_space=pl.ANY)] * 9,
        out_specs=pl.BlockSpec(memory_space=pltpu.VMEM),
        scratch_shapes=[
            held(N, B, jnp.int32), held(F, F), held(F, F), held(F, F), held(F, F), held(2 * B, HD, f32),
            held(PROMPT), held(PROMPT), held(F, F), held(F, F),
            held(N * B, F), held(N * B, F), held(N * B, F),
            held(8 * HALF), held(8 * HALF), held(HALF), held(HALF),
            held(16 * HALF), held(16 * HALF), held(2 * HALF), held(2 * HALF),
            held(HALF, PROMPT, f32), held(HALF + B), held(HALF + B),
            held(HALF), held(8 * HALF), held(N * B, F), held(N * B, F),
            pltpu.SemaphoreType.DMA((9,)),
            pltpu.SemaphoreType.DMA((15,)),
            pltpu.SemaphoreType.DMA((15,)),
        ],
        compiler_params=pltpu.CompilerParams(
            collective_id=0, has_side_effects=True, vmem_limit_bytes=62 * 1024 * 1024
        ),
    )(gen_ids, embed_rows, w_query, w_key, w_value, w_out, prompt_keys, prompt_values, table)


def solution(mesh):
    return jax.shard_map(
        body,
        mesh=mesh,
        in_specs=(
            P(), P("head", "seq"), P("seq", "head"), P("seq", "head"), P("seq", "head"),
            P("head", "seq"), P("seq", "head"), P("seq", "head"),
        ),
        out_specs=P("seq", "head"),
        check_vma=False,
    )
```

time: 94.7 us -> 63 us (0.67)
  the two profiles are of different devices: /device:TPU:25 before, /device:TPU:64 now
where the time goes in v2:
time: 63 us; the launch traced here: 62.5 us
  Pallas kernels  61.2 us (97%)
  local copies, waits for them, and re-layouts  1.32 us (2%)
    pallas_call x1, Pallas kernels, body(): pl.pallas_call(kernel, out_shape=jax.ShapeDtypeStruct((B, F), bf16), in_s...  61.2 us
    unnamed x1, local copies, waits for them, and re-layouts  1.32 us

profile of v2, /device:TPU:64, one launch (start us, length us, event | category | flops | bytes accessed | tf_op | source)
XLA Modules:
  0.0 62.5 jit_solution(9129046754443905416)
XLA Ops:
  0.0 61.2 %shard_map.91 = bf16[16,512]{1,0:T(8,128)(2,1)} custom-call(s32[16,16]{1,0:T(8,128)} %ids_hbm.1, bf16[512,512]{1,0:T(8,128)(2,1)} %e_hbm.1, bf16[512,512]{1,0:T(8,128)(2,1)} %wq_hbm.1, bf16[512,512]{1,0:T(8,128)(2,1)} %wk_hbm.1, bf16[512,512]{1,0:T(8,128)(2,1)} %wv_hbm.1, bf16[512,512]{1,0:T(8,128)(2,1)} %wo_hbm.1, bf16[512,512]{1,0:T(8,128)(2,1)} %k_hbm.1, ...), custom_call_target="tpu_custom_call" | custom-call | tf_op jit(solution)/shard_map/pallas_call | solution.py:357
  61.2 1.3 %copy.11 = bf16[16,512]{1,0:T(8,128)(2,1)} copy(bf16[16,512]{1,0:T(8,128)(2,1)} %shard_map.91) | data formatting | bytes 32768

commit v3 on v2

v3 whole, which is shorter than its diff:
```python
import math

import jax
import jax.numpy as jnp
import numpy as np
from jax import lax
from jax.experimental import pallas as pl
from jax.experimental.pallas import tpu as pltpu
from jax.sharding import PartitionSpec as P

MESH = pl.DeviceIdType.MESH
HD = 128
N = 16
B = 16
F = 512
CH = N * B // 2
HALF = CH
Q = CH // 2
YS = 4
PROMPT = 8 * F
CHUNK = 1024
EXP_SCALE = math.log2(math.e) / math.sqrt(HD)
f32 = jnp.float32
bf16 = jnp.bfloat16
EMB_RS, K_MOVE, V_MOVE, K_PAIR, V_PAIR, KV_RS, KV_Z, W_MOVE, W_TURN, OUT_RS, KV_PAIR = range(11)
EMB_AG, Q_RS, Q_Z, O_Z, ATT_AG = range(11, 21, 2)


def part(index, size):
    return pl.ds(pl.multiple_of(index * size, size), size)


def rounded(x):
    return x.astype(bf16).astype(f32)


def slot_sum(ref, slots, rows):
    return jnp.sum(ref[...].astype(f32).reshape(slots, rows, ref.shape[-1]), axis=0)


def turned(x, cosine, sine):
    return x * cosine + pltpu.roll(x, HD // 2, 1) * sine


def kernel(
    ids_hbm, e_hbm, wq_hbm, wk_hbm, wv_hbm, wo_hbm, k_hbm, v_hbm, tab_hbm, out_ref,
    ids, emb, wq, wk, wv, tab, keys, values, w_stage, w_all,
    pick, r_emb, x_all, q_part, r_q, q_mine, q_other, kv_part, kv_far, r_kv, kv_mine, kv_other,
    scores, o_mine, o_other, att, att_all, out_part, r_out,
    load_sem, send_sem, recv_sem,
):
    s = lax.axis_index("seq")
    h = lax.axis_index("head")
    y, zh, c = s // 4, lax.rem(s // 2, 2), lax.rem(s, 2)
    x, zl = h // 4, lax.rem(h, 4)
    sibling = (s + 1 - 2 * c, h)
    antipode = (s + 2 - 4 * zh, h)
    pos = y * 2 + c
    own = lax.rem(s, 4)
    out_self = own == zl

    loads = [
        pltpu.make_async_copy(src, dst, load_sem.at[i])
        for i, (src, dst) in enumerate(
            [
                (ids_hbm, ids), (e_hbm, emb), (wq_hbm, wq), (wk_hbm, wk), (wv_hbm, wv), (tab_hbm, tab),
                (k_hbm.at[:, part(y, HD)], keys.at[part(c * YS + y, F)]),
                (v_hbm.at[:, part(y, HD)], values.at[part(c * YS + y, F)]),
                (wo_hbm.at[part(y, HD)], w_stage.at[part(y, HD)]),
            ]
        )
    ]
    for load in loads:
        load.start()

    barrier = pltpu.get_barrier_semaphore()

    def greet(device):
        pl.semaphore_signal(barrier, inc=1, device_id=device, device_id_type=MESH)

    def in_group(e):
        return ((e // 2) * 4 + zh * 2 + lax.rem(e, 2), h)

    def greet_plane(d, carry):
        greet((s, lax.rem(h + d, N)))
        return carry

    def greet_group(d, carry):
        greet(in_group(lax.rem(pos + d, 8)))
        return carry

    lax.fori_loop(1, N, greet_plane, 0)
    greet(antipode)
    lax.fori_loop(1, 8, greet_group, 0)

    def copy(i, src, dst, device):
        return pltpu.make_async_remote_copy(
            src_ref=src, dst_ref=dst, send_sem=send_sem.at[i], recv_sem=recv_sem.at[i],
            device_id=device, device_id_type=MESH,
        )

    def rows(i, ref, count):
        return copy(i, ref.at[pl.ds(0, count)], ref.at[pl.ds(0, count)], sibling)

    loads[0].wait()
    shifted = (ids[...] - h * F).astype(f32)
    eye = lax.broadcasted_iota(jnp.int32, (B, B), 0) == lax.broadcasted_iota(jnp.int32, (B, B), 1)
    entry = lax.broadcasted_iota(jnp.int32, (B, F), 1).astype(f32)
    selectors = []
    for k in range(2):
        chosen = []
        for b in range(8):
            t = (b % 4) * 4 + k * 2 + b // 4
            row = jnp.broadcast_to(shifted[t : t + 1, :], (B, B))
            column = jnp.sum(jnp.where(eye, row, 0.0), axis=1, keepdims=True)
            chosen.append(jnp.where(column == entry, 1.0, 0.0).astype(bf16))
        selectors.append(jnp.concatenate(chosen, axis=0))
    loads[1].wait()
    pick[:CH, :] = jnp.dot(selectors[0], emb[...], preferred_element_type=f32).astype(bf16)

    pl.semaphore_wait(barrier, 15 + 7 + 1)

    mine_k = lax.rem(h, 2)
    mine = mine_k * 8 + h // 2
    for k in range(2):
        if k:
            pick[CH:, :] = jnp.dot(selectors[1], emb[...], preferred_element_type=f32).astype(bf16)

        def send_pick(d, carry, k=k):
            b = lax.rem(h // 2 + d, 8)

            @pl.when((d > 0) | (mine_k != k))
            def _():
                copy(EMB_RS, pick.at[part(k * 8 + b, B)], r_emb.at[part(h, B)], (s, 2 * b + k)).start()

            return carry

        lax.fori_loop(0, 8, send_pick, 0)
    r_emb[part(h, B), :] = pick[part(mine, B), :]

    def move_prompt(d, carry):
        j = lax.rem(y + d, YS)
        device = (j * 4 + zh * 2 + c, h)
        slot = part(c * YS + y, F)
        copy(K_MOVE, k_hbm.at[:, part(j, HD)], keys.at[slot], device).start()
        copy(V_MOVE, v_hbm.at[:, part(j, HD)], values.at[slot], device).start()
        return carry

    lax.fori_loop(1, YS, move_prompt, 0)

    def move_w(d, carry):
        j = lax.rem(y + d, YS)
        device = (j * 4 + zh * 2 + c, h)
        copy(W_MOVE, wo_hbm.at[part(j, HD)], w_stage.at[part(y, HD)], device).start()
        return carry

    lax.fori_loop(1, YS, move_w, 0)

    rows(EMB_RS, r_emb, 15 * B).wait_recv()
    x_all[part(mine, B), :] = slot_sum(r_emb, N, B).astype(bf16)

    def send_x(d, carry):
        copy(EMB_AG + mine_k, x_all.at[part(mine, B)], x_all.at[part(mine, B)], (s, lax.rem(h + d, N))).start()
        return carry

    lax.fori_loop(1, N, send_x, 0)
    loads[2].wait()

    for k in range(2):
        @pl.when(mine_k == k)
        def _(k=k):
            rows(EMB_AG + k, x_all, 7 * B).wait_recv()

        @pl.when(mine_k != k)
        def _(k=k):
            rows(EMB_AG + k, x_all, 8 * B).wait_recv()

        projected = jnp.dot(x_all[k * CH : (k + 1) * CH, :], wq[...], preferred_element_type=f32).astype(bf16)
        for e in range(8):
            q_part[(k * 8 + e) * Q : (k * 8 + e + 1) * Q, :] = projected[
                (e % 2) * Q : (e % 2 + 1) * Q, (e // 2) * HD : (e // 2 + 1) * HD
            ]

        def send_q(d, carry, k=k):
            e = lax.rem(pos + d, 8)
            copy(Q_RS + k, q_part.at[part(k * 8 + e, Q)], r_q.at[part(k * 8 + pos, Q)], in_group(e)).start()
            return carry

        lax.fori_loop(1, 8, send_q, 0)
        r_q[part(k * 8 + pos, Q), :] = q_part[part(k * 8 + pos, Q), :]

    loads[3].wait()
    loads[4].wait()
    for i, w in enumerate((wk, wv)):
        projected = jnp.dot(x_all[...], w[...], preferred_element_type=f32).astype(bf16)
        for e in range(8):
            for k in range(2):
                first = (((e % 2) * YS + e // 2) * 2 + i) * HALF + k * Q
                row = k * CH + (e % 2) * Q
                kv_part[first : first + Q, :] = projected[row : row + Q, (e // 2) * HD : (e // 2 + 1) * HD]
    copy(KV_PAIR, kv_part.at[part(1 - c, 8 * HALF)], kv_far, sibling).start()

    loads[6].wait()
    loads[7].wait()
    rows(K_MOVE, keys, 3 * F).wait_recv()
    rows(V_MOVE, values, 3 * F).wait_recv()
    pair_rows = part(c, PROMPT // 2)
    copy(K_PAIR, keys.at[pair_rows], keys.at[pair_rows], sibling).start()
    copy(V_PAIR, values.at[pair_rows], values.at[pair_rows], sibling).start()

    rows(KV_PAIR, kv_far, 8 * HALF).wait_recv()
    kv_far[...] = (kv_part[part(c, 8 * HALF), :].astype(f32) + kv_far[...].astype(f32)).astype(bf16)

    def send_kv(d, carry):
        j = lax.rem(y + d, YS)
        device = (j * 4 + zh * 2 + c, h)
        copy(KV_RS, kv_far.at[part(j, 2 * HALF)], r_kv.at[part(y, 2 * HALF)], device).start()
        return carry

    lax.fori_loop(1, YS, send_kv, 0)
    r_kv[part(y, 2 * HALF), :] = kv_far[part(y, 2 * HALF), :]

    q_sums = []
    for k in range(2):
        rows(Q_RS + k, r_q, 7 * Q).wait_recv()
        q_sums.append(jnp.sum(r_q[k * 8 * Q : (k + 1) * 8 * Q, :].astype(f32).reshape(8, Q, HD), axis=0))
        q_mine[k * Q : (k + 1) * Q, :] = q_sums[k].astype(bf16)
        copy(Q_Z + k, q_mine.at[part(k, Q)], q_other.at[part(k, Q)], antipode).start()

    rows(KV_RS, r_kv, 6 * HALF).wait_recv()
    kv_sum = slot_sum(r_kv, YS, 2 * HALF)
    kv_mine[...] = kv_sum.astype(bf16)
    copy(KV_Z, kv_mine, kv_other, antipode).start()

    loads[8].wait()
    rows(W_MOVE, w_stage, 3 * HD).wait_recv()

    def turn_w(d, carry):
        i = lax.rem(x + d, 4)
        copy(W_TURN, w_stage.at[part(i, HD)], w_all.at[part(x, HD)], (s, 4 * i + zl)).start()
        return carry

    lax.fori_loop(1, 4, turn_w, 0)
    w_all[part(x, HD), :] = w_stage[part(x, HD), :]

    loads[5].wait()
    cosine = jnp.concatenate([tab[:B, :]] * 8, axis=0)
    sine = jnp.concatenate([tab[B:, :]] * 8, axis=0)
    lane = lax.broadcasted_iota(jnp.int32, (Q, HD), 1)
    found = []
    for k in range(2):
        rows(Q_Z + k, q_other, Q).wait_recv()
        total = q_sums[k] + q_other[k * Q : (k + 1) * Q, :].astype(f32)
        queries = turned(total, cosine[:Q], sine[:Q]).astype(bf16)
        if k == 0:
            rows(K_PAIR, keys, PROMPT // 2).wait_recv()
        peak = None
        for i in range(PROMPT // CHUNK):
            block = lax.dot_general(
                queries, keys[i * CHUNK : (i + 1) * CHUNK, :], (((1,), (1,)), ((), ())), preferred_element_type=f32
            )
            scores[k * Q : (k + 1) * Q, i * CHUNK : (i + 1) * CHUNK] = block
            top = jnp.max(block, axis=1, keepdims=True)
            peak = top if peak is None else jnp.maximum(peak, top)
        if k == 0:
            rows(V_PAIR, values, PROMPT // 2).wait_recv()
        weight_sum = jnp.zeros((Q, 1), f32)
        summed = jnp.zeros((Q, HD), f32)
        for i in range(PROMPT // CHUNK):
            weights = jnp.exp2((scores[k * Q : (k + 1) * Q, i * CHUNK : (i + 1) * CHUNK] - peak) * EXP_SCALE)
            weight_sum += jnp.sum(weights, axis=1, keepdims=True)
            summed += jnp.dot(
                weights.astype(bf16), values[i * CHUNK : (i + 1) * CHUNK, :], preferred_element_type=f32
            )
        high = rounded(peak)
        middle = rounded(peak - high)
        sum_high = rounded(weight_sum)
        packed = jnp.zeros((Q, HD), f32)
        for i, stat in enumerate(
            (high, middle, rounded(peak - high - middle), sum_high, rounded(weight_sum - sum_high))
        ):
            packed = jnp.where(lane == i, stat, packed)
        packed = jnp.concatenate([packed, jnp.zeros((HD - Q, HD), f32)], axis=0)
        first = k * (Q + B)
        o_mine[first : first + Q, :] = summed.astype(bf16)
        o_mine[first + Q : first + Q + B, :] = packed.T[:B, :].astype(bf16)
        copy(O_Z + k, o_mine.at[part(k, Q + B)], o_other.at[part(k, Q + B)], antipode).start()
        found.append((queries, peak, weight_sum, summed))

    rows(KV_Z, kv_other, 2 * HALF).wait_recv()
    both = kv_sum + kv_other[...].astype(f32)
    own_keys = turned(both[:HALF], cosine, sine).astype(bf16)
    own_values = both[HALF:].astype(bf16)
    queries = jnp.concatenate([found[0][0], found[1][0]], axis=0)
    own_scores = lax.dot_general(queries, own_keys, (((1,), (1,)), ((), ())), preferred_element_type=f32)
    token = lax.broadcasted_iota(jnp.int32, (HALF, HALF), 0)
    other = lax.broadcasted_iota(jnp.int32, (HALF, HALF), 1)
    seen = (token // B == other // B) & (other <= token)
    own_scores = jnp.where(seen, own_scores, -jnp.inf)
    own_peak = jnp.max(own_scores, axis=1, keepdims=True)
    own_weights = jnp.exp2((own_scores - own_peak) * EXP_SCALE)
    own_sum = jnp.sum(own_weights, axis=1, keepdims=True)
    own_out = jnp.dot(own_weights.astype(bf16), own_values, preferred_element_type=f32)

    place = x * 2 + c
    for k in range(2):
        rows(O_Z + k, o_other, Q + B).wait_recv()
        _, peak, weight_sum, summed = found[k]
        here = slice(k * Q, (k + 1) * Q)
        first = k * (Q + B)
        stats = o_other[first + Q : first + Q + B, :].astype(f32).T[:Q, :]
        far_peak = stats[:, 0:1] + stats[:, 1:2] + stats[:, 2:3]
        far_sum = stats[:, 3:4] + stats[:, 4:5]
        top = jnp.maximum(jnp.maximum(peak, own_peak[here]), far_peak)
        near = jnp.exp2((peak - top) * EXP_SCALE)
        far = jnp.exp2((far_peak - top) * EXP_SCALE)
        own_factor = jnp.exp2((own_peak[here] - top) * EXP_SCALE)
        total = near * weight_sum + far * far_sum + own_factor * own_sum[here]
        joined = near * summed + far * o_other[first : first + Q, :].astype(f32) + own_factor * own_out[here]
        att[here, :] = (joined / total).astype(bf16)

        def send_att(d, carry, k=k):
            e = lax.rem(place + d, 8)
            device = (s - c + lax.rem(e, 2), (e // 2) * 4 + zl)
            copy(ATT_AG + k, att.at[part(k, Q)], att_all.at[part(k * 8 + place, Q)], device).start()
            return carry

        lax.fori_loop(1, 8, send_att, 0)
        att_all[part(k * 8 + place, Q), :] = att[here, :]

    rows(W_TURN, w_all, 3 * HD).wait_recv()
    out_slot = part(y * 4 + zl, B)
    for k in range(2):
        rows(ATT_AG + k, att_all, 7 * Q).wait_recv()
        attended = jnp.concatenate(
            [
                jnp.concatenate(
                    [att_all[(k * 8 + i * 2 + e) * Q : (k * 8 + i * 2 + e + 1) * Q, :] for i in range(4)], axis=1
                )
                for e in range(2)
            ],
            axis=0,
        )
        out_part[k * CH : (k + 1) * CH, :] = jnp.dot(
            attended, w_all[...], preferred_element_type=f32
        ).astype(bf16)

        def send_out(d, carry, k=k):
            e = lax.rem(pos + d, 8)
            block = k * 8 + lax.rem(e, 2) * 4 + e // 2
            device = ((e // 2) * 4 + k * 2 + lax.rem(e, 2), 4 * x + own)

            @pl.when((d > 0) | (zh != k) | jnp.logical_not(out_self))
            def _():
                copy(OUT_RS, out_part.at[part(block, B)], r_out.at[out_slot], device).start()

            return carry

        lax.fori_loop(0, 8, send_out, 0)

    @pl.when(out_self)
    def _():
        r_out[out_slot, :] = out_part[part(zh * 8 + c * 4 + y, B), :]
        rows(OUT_RS, r_out, 15 * B).wait_recv()

    @pl.when(jnp.logical_not(out_self))
    def _():
        rows(OUT_RS, r_out, 16 * B).wait_recv()

    out_ref[...] = slot_sum(r_out, N, B).astype(bf16)

    rows(EMB_RS, pick, 15 * B).wait_send()
    rows(EMB_AG + mine_k, x_all, 15 * B).wait_send()
    rows(K_MOVE, keys, 3 * F).wait_send()
    rows(V_MOVE, values, 3 * F).wait_send()
    rows(W_MOVE, w_stage, 3 * HD).wait_send()
    rows(K_PAIR, keys, PROMPT // 2).wait_send()
    rows(V_PAIR, values, PROMPT // 2).wait_send()
    for k in range(2):
        rows(Q_RS + k, q_part, 7 * Q).wait_send()
        rows(Q_Z + k, q_mine, Q).wait_send()
        rows(O_Z + k, o_mine, Q + B).wait_send()
        rows(ATT_AG + k, att_all, 7 * Q).wait_send()
    rows(KV_PAIR, kv_part, 8 * HALF).wait_send()
    rows(KV_RS, kv_far, 6 * HALF).wait_send()
    rows(KV_Z, kv_mine, 2 * HALF).wait_send()
    rows(W_TURN, w_stage, 3 * HD).wait_send()

    @pl.when(out_self)
    def _():
        rows(OUT_RS, out_part, 15 * B).wait_send()

    @pl.when(jnp.logical_not(out_self))
    def _():
        rows(OUT_RS, out_part, 16 * B).wait_send()


def rotation_table(first, count):
    half = HD // 2
    frequency = 10000.0 ** (-np.arange(half, dtype=np.float64) / half)
    angles = (first + np.arange(count, dtype=np.float64))[:, None] * frequency[None, :]
    cosine, sine = np.cos(angles), np.sin(angles)
    return np.concatenate(
        [np.concatenate([cosine, cosine], 1), np.concatenate([-sine, sine], 1)], 0
    ).astype(np.float32)


def body(gen_ids, embed_rows, w_query, w_key, w_value, w_out, prompt_keys, prompt_values):
    table = jnp.asarray(rotation_table(prompt_keys.shape[0] * N, B))

    def held(count, width=HD, dtype=bf16):
        return pltpu.VMEM((count, width), dtype)

    return pl.pallas_call(
        kernel,
        out_shape=jax.ShapeDtypeStruct((B, F), bf16),
        in_specs=[pl.BlockSpec(memory_space=pl.ANY)] * 9,
        out_specs=pl.BlockSpec(memory_space=pltpu.VMEM),
        scratch_shapes=[
            held(N, B, jnp.int32), held(F, F), held(F, F), held(F, F), held(F, F), held(2 * B, HD, f32),
            held(PROMPT), held(PROMPT), held(F, F), held(F, F),
            held(N * B, F), held(N * B, F), held(N * B, F),
            held(8 * HALF), held(8 * HALF), held(HALF), held(HALF),
            held(16 * HALF), held(8 * HALF), held(8 * HALF), held(2 * HALF), held(2 * HALF),
            held(HALF, PROMPT, f32), held(HALF + 2 * B), held(HALF + 2 * B),
            held(HALF), held(8 * HALF), held(N * B, F), held(N * B, F),
            pltpu.SemaphoreType.DMA((9,)),
            pltpu.SemaphoreType.DMA((21,)),
            pltpu.SemaphoreType.DMA((21,)),
        ],
        compiler_params=pltpu.CompilerParams(
            collective_id=0, has_side_effects=True, vmem_limit_bytes=62 * 1024 * 1024
        ),
    )(gen_ids, embed_rows, w_query, w_key, w_value, w_out, prompt_keys, prompt_values, table)


def solution(mesh):
    return jax.shard_map(
        body,
        mesh=mesh,
        in_specs=(
            P(), P("head", "seq"), P("seq", "head"), P("seq", "head"), P("seq", "head"),
            P("head", "seq"), P("seq", "head"), P("seq", "head"),
        ),
        out_specs=P("seq", "head"),
        check_vma=False,
    )
```

time: 63 us -> 59.4 us (0.943)
  Pallas kernels: 61.2 us -> 57.5 us
    pallas_call x1, Pallas kernels: 61.2 us -> 57.5 us  [body(): pl.pallas_call(kernel, out_shape=jax.ShapeDtypeStruct((B, F), bf16), in_s...]
where the time goes in v3:
time: 59.4 us; the launch traced here: 58.8 us
  Pallas kernels  57.5 us (97%)
  local copies, waits for them, and re-layouts  1.32 us (2%)
    pallas_call x1, Pallas kernels, body(): pl.pallas_call(kernel, out_shape=jax.ShapeDtypeStruct((B, F), bf16), in_s...  57.5 us
    unnamed x1, local copies, waits for them, and re-layouts  1.32 us

profile of v3, /device:TPU:64, one launch (start us, length us, event | category | flops | bytes accessed | tf_op | source)
XLA Modules:
  0.0 58.8 jit_solution(18402024737371223880)
XLA Ops:
  0.0 57.5 %shard_map.91 = bf16[16,512]{1,0:T(8,128)(2,1)} custom-call(s32[16,16]{1,0:T(8,128)} %ids_hbm.1, bf16[512,512]{1,0:T(8,128)(2,1)} %e_hbm.1, bf16[512,512]{1,0:T(8,128)(2,1)} %wq_hbm.1, bf16[512,512]{1,0:T(8,128)(2,1)} %wk_hbm.1, bf16[512,512]{1,0:T(8,128)(2,1)} %wv_hbm.1, bf16[512,512]{1,0:T(8,128)(2,1)} %wo_hbm.1, bf16[512,512]{1,0:T(8,128)(2,1)} %k_hbm.1, ...), custom_call_target="tpu_custom_call" | custom-call | tf_op jit(solution)/shard_map/pallas_call | solution.py:414
  57.5 1.3 %copy.11 = bf16[16,512]{1,0:T(8,128)(2,1)} copy(bf16[16,512]{1,0:T(8,128)(2,1)} %shard_map.91) | data formatting | bytes 32768

commit v4 on v3

--- a/solution.py
+++ b/solution.py
@@ -78,6 +78,9 @@
     def greet(device):
         pl.semaphore_signal(barrier, inc=1, device_id=device, device_id_type=MESH)
 
+    def far_first(base, core):
+        return [2 * lax.rem(base + d, 4) + lax.rem(core + e, 2) for d in (2, 1, 3, 0) for e in (1, 0)]
+
     def in_group(e):
         return ((e // 2) * 4 + zh * 2 + lax.rem(e, 2), h)
 
@@ -120,24 +123,6 @@
 
     pl.semaphore_wait(barrier, 15 + 7 + 1)
 
-    mine_k = lax.rem(h, 2)
-    mine = mine_k * 8 + h // 2
-    for k in range(2):
-        if k:
-            pick[CH:, :] = jnp.dot(selectors[1], emb[...], preferred_element_type=f32).astype(bf16)
-
-        def send_pick(d, carry, k=k):
-            b = lax.rem(h // 2 + d, 8)
-
-            @pl.when((d > 0) | (mine_k != k))
-            def _():
-                copy(EMB_RS, pick.at[part(k * 8 + b, B)], r_emb.at[part(h, B)], (s, 2 * b + k)).start()
-
-            return carry
-
-        lax.fori_loop(0, 8, send_pick, 0)
-    r_emb[part(h, B), :] = pick[part(mine, B), :]
-
     def move_prompt(d, carry):
         j = lax.rem(y + d, YS)
         device = (j * 4 + zh * 2 + c, h)
@@ -156,14 +141,29 @@
 
     lax.fori_loop(1, YS, move_w, 0)
 
+    mine_k = lax.rem(h, 2)
+    mine = mine_k * 8 + h // 2
+    for k in range(2):
+        if k:
+            pick[CH:, :] = jnp.dot(selectors[1], emb[...], preferred_element_type=f32).astype(bf16)
+
+        for d in (2, 1, 3, 0):
+            for far in (1 - zl // 2, zl // 2):
+                j = lax.rem(x + d, 4) * 4 + 2 * far + k
+                send = copy(EMB_RS, pick.at[part(k * 8 + j // 2, B)], r_emb.at[part(h, B)], (s, j))
+                if d:
+                    send.start()
+                else:
+                    pl.when(j != h)(send.start)
+    r_emb[part(h, B), :] = pick[part(mine, B), :]
+
     rows(EMB_RS, r_emb, 15 * B).wait_recv()
     x_all[part(mine, B), :] = slot_sum(r_emb, N, B).astype(bf16)
 
-    def send_x(d, carry):
-        copy(EMB_AG + mine_k, x_all.at[part(mine, B)], x_all.at[part(mine, B)], (s, lax.rem(h + d, N))).start()
-        return carry
-
-    lax.fori_loop(1, N, send_x, 0)
+    for d in (2, 1, 3, 0):
+        for z in (3 - zl, lax.rem(zl + 2, 4), zl + 1 - 2 * lax.rem(zl, 2), zl)[: 4 if d else 3]:
+            device = (s, lax.rem(x + d, 4) * 4 + z)
+            copy(EMB_AG + mine_k, x_all.at[part(mine, B)], x_all.at[part(mine, B)], device).start()
     loads[2].wait()
 
     for k in range(2):
@@ -181,12 +181,8 @@
                 (e % 2) * Q : (e % 2 + 1) * Q, (e // 2) * HD : (e // 2 + 1) * HD
             ]
 
-        def send_q(d, carry, k=k):
-            e = lax.rem(pos + d, 8)
+        for e in far_first(y, c)[:7]:
             copy(Q_RS + k, q_part.at[part(k * 8 + e, Q)], r_q.at[part(k * 8 + pos, Q)], in_group(e)).start()
-            return carry
-
-        lax.fori_loop(1, 8, send_q, 0)
         r_q[part(k * 8 + pos, Q), :] = q_part[part(k * 8 + pos, Q), :]
 
     loads[3].wait()
@@ -200,6 +196,25 @@
                 kv_part[first : first + Q, :] = projected[row : row + Q, (e // 2) * HD : (e // 2 + 1) * HD]
     copy(KV_PAIR, kv_part.at[part(1 - c, 8 * HALF)], kv_far, sibling).start()
 
+    rows(KV_PAIR, kv_far, 8 * HALF).wait_recv()
+    kv_far[...] = (kv_part[part(c, 8 * HALF), :].astype(f32) + kv_far[...].astype(f32)).astype(bf16)
+
+    def send_kv(d, carry):
+        j = lax.rem(y + d, YS)
+        device = (j * 4 + zh * 2 + c, h)
+        copy(KV_RS, kv_far.at[part(j, 2 * HALF)], r_kv.at[part(y, 2 * HALF)], device).start()
+        return carry
+
+    lax.fori_loop(1, YS, send_kv, 0)
+    r_kv[part(y, 2 * HALF), :] = kv_far[part(y, 2 * HALF), :]
+
+    q_sums = []
+    for k in range(2):
+        rows(Q_RS + k, r_q, 7 * Q).wait_recv()
+        q_sums.append(jnp.sum(r_q[k * 8 * Q : (k + 1) * 8 * Q, :].astype(f32).reshape(8, Q, HD), axis=0))
+        q_mine[k * Q : (k + 1) * Q, :] = q_sums[k].astype(bf16)
+        copy(Q_Z + k, q_mine.at[part(k, Q)], q_other.at[part(k, Q)], antipode).start()
+
     loads[6].wait()
     loads[7].wait()
     rows(K_MOVE, keys, 3 * F).wait_recv()
@@ -208,40 +223,21 @@
     copy(K_PAIR, keys.at[pair_rows], keys.at[pair_rows], sibling).start()
     copy(V_PAIR, values.at[pair_rows], values.at[pair_rows], sibling).start()
 
-    rows(KV_PAIR, kv_far, 8 * HALF).wait_recv()
-    kv_far[...] = (kv_part[part(c, 8 * HALF), :].astype(f32) + kv_far[...].astype(f32)).astype(bf16)
-
-    def send_kv(d, carry):
-        j = lax.rem(y + d, YS)
-        device = (j * 4 + zh * 2 + c, h)
-        copy(KV_RS, kv_far.at[part(j, 2 * HALF)], r_kv.at[part(y, 2 * HALF)], device).start()
-        return carry
-
-    lax.fori_loop(1, YS, send_kv, 0)
-    r_kv[part(y, 2 * HALF), :] = kv_far[part(y, 2 * HALF), :]
-
-    q_sums = []
-    for k in range(2):
-        rows(Q_RS + k, r_q, 7 * Q).wait_recv()
-        q_sums.append(jnp.sum(r_q[k * 8 * Q : (k + 1) * 8 * Q, :].astype(f32).reshape(8, Q, HD), axis=0))
-        q_mine[k * Q : (k + 1) * Q, :] = q_sums[k].astype(bf16)
-        copy(Q_Z + k, q_mine.at[part(k, Q)], q_other.at[part(k, Q)], antipode).start()
+    loads[8].wait()
+    rows(W_MOVE, w_stage, 3 * HD).wait_recv()
+
+    def turn_w(d, carry):
+        i = lax.rem(x + d, 4)
+        copy(W_TURN, w_stage.at[part(i, HD)], w_all.at[part(x, HD)], (s, 4 * i + zl)).start()
+        return carry
+
+    lax.fori_loop(1, 4, turn_w, 0)
+    w_all[part(x, HD), :] = w_stage[part(x, HD), :]
 
     rows(KV_RS, r_kv, 6 * HALF).wait_recv()
     kv_sum = slot_sum(r_kv, YS, 2 * HALF)
     kv_mine[...] = kv_sum.astype(bf16)
     copy(KV_Z, kv_mine, kv_other, antipode).start()
-
-    loads[8].wait()
-    rows(W_MOVE, w_stage, 3 * HD).wait_recv()
-
-    def turn_w(d, carry):
-        i = lax.rem(x + d, 4)
-        copy(W_TURN, w_stage.at[part(i, HD)], w_all.at[part(x, HD)], (s, 4 * i + zl)).start()
-        return carry
-
-    lax.fori_loop(1, 4, turn_w, 0)
-    w_all[part(x, HD), :] = w_stage[part(x, HD), :]
 
     loads[5].wait()
     cosine = jnp.concatenate([tab[:B, :]] * 8, axis=0)
@@ -319,13 +315,9 @@
         joined = near * summed + far * o_other[first : first + Q, :].astype(f32) + own_factor * own_out[here]
         att[here, :] = (joined / total).astype(bf16)
 
-        def send_att(d, carry, k=k):
-            e = lax.rem(place + d, 8)
+        for e in far_first(x, c)[:7]:
             device = (s - c + lax.rem(e, 2), (e // 2) * 4 + zl)
             copy(ATT_AG + k, att.at[part(k, Q)], att_all.at[part(k * 8 + place, Q)], device).start()
-            return carry
-
-        lax.fori_loop(1, 8, send_att, 0)
         att_all[part(k * 8 + place, Q), :] = att[here, :]
 
     rows(W_TURN, w_all, 3 * HD).wait_recv()
@@ -345,29 +337,14 @@
             attended, w_all[...], preferred_element_type=f32
         ).astype(bf16)
 
-        def send_out(d, carry, k=k):
-            e = lax.rem(pos + d, 8)
+        for n, e in enumerate(far_first(y, c)):
             block = k * 8 + lax.rem(e, 2) * 4 + e // 2
             device = ((e // 2) * 4 + k * 2 + lax.rem(e, 2), 4 * x + own)
-
-            @pl.when((d > 0) | (zh != k) | jnp.logical_not(out_self))
-            def _():
-                copy(OUT_RS, out_part.at[part(block, B)], r_out.at[out_slot], device).start()
-
-            return carry
-
-        lax.fori_loop(0, 8, send_out, 0)
-
-    @pl.when(out_self)
-    def _():
-        r_out[out_slot, :] = out_part[part(zh * 8 + c * 4 + y, B), :]
-        rows(OUT_RS, r_out, 15 * B).wait_recv()
-
-    @pl.when(jnp.logical_not(out_self))
-    def _():
-        rows(OUT_RS, r_out, 16 * B).wait_recv()
-
-    out_ref[...] = slot_sum(r_out, N, B).astype(bf16)
+            send = copy(OUT_RS, out_part.at[part(block, B)], r_out.at[out_slot], device)
+            if n < 7:
+                send.start()
+            else:
+                pl.when((zh != k) | jnp.logical_not(out_self))(send.start)
 
     rows(EMB_RS, pick, 15 * B).wait_send()
     rows(EMB_AG + mine_k, x_all, 15 * B).wait_send()
@@ -385,6 +362,18 @@
     rows(KV_RS, kv_far, 6 * HALF).wait_send()
     rows(KV_Z, kv_mine, 2 * HALF).wait_send()
     rows(W_TURN, w_stage, 3 * HD).wait_send()
+
+
+    @pl.when(out_self)
+    def _():
+        r_out[out_slot, :] = out_part[part(zh * 8 + c * 4 + y, B), :]
+        rows(OUT_RS, r_out, 15 * B).wait_recv()
+
+    @pl.when(jnp.logical_not(out_self))
+    def _():
+        rows(OUT_RS, r_out, 16 * B).wait_recv()
+
+    out_ref[...] = slot_sum(r_out, N, B).astype(bf16)
 
     @pl.when(out_self)
     def _():

time: 59.4 us -> 58.2 us (0.980)
  Pallas kernels: 57.5 us -> 56.6 us
    pallas_call x1, Pallas kernels: 57.5 us -> 56.6 us  [body(): pl.pallas_call(kernel, out_shape=jax.ShapeDtypeStruct((B, F), bf16), in_s...]
where the time goes in v4:
time: 58.2 us; the launch traced here: 58 us
  Pallas kernels  56.6 us (97%)
  local copies, waits for them, and re-layouts  1.32 us (2%)
    pallas_call x1, Pallas kernels, body(): pl.pallas_call(kernel, out_shape=jax.ShapeDtypeStruct((B, F), bf16), in_s...  56.6 us
    unnamed x1, local copies, waits for them, and re-layouts  1.32 us

profile of v4, /device:TPU:64, one launch (start us, length us, event | category | flops | bytes accessed | tf_op | source)
XLA Modules:
  0.0 58.0 jit_solution(14072569955571458575)
XLA Ops:
  0.0 56.6 %shard_map.91 = bf16[16,512]{1,0:T(8,128)(2,1)} custom-call(s32[16,16]{1,0:T(8,128)} %ids_hbm.1, bf16[512,512]{1,0:T(8,128)(2,1)} %e_hbm.1, bf16[512,512]{1,0:T(8,128)(2,1)} %wq_hbm.1, bf16[512,512]{1,0:T(8,128)(2,1)} %wk_hbm.1, bf16[512,512]{1,0:T(8,128)(2,1)} %wv_hbm.1, bf16[512,512]{1,0:T(8,128)(2,1)} %wo_hbm.1, bf16[512,512]{1,0:T(8,128)(2,1)} %k_hbm.1, ...), custom_call_target="tpu_custom_call" | custom-call | tf_op jit(solution)/shard_map/pallas_call | solution.py:403
  56.6 1.3 %copy.11 = bf16[16,512]{1,0:T(8,128)(2,1)} copy(bf16[16,512]{1,0:T(8,128)(2,1)} %shard_map.91) | data formatting | bytes 32768

commit v5 on v4

--- a/solution.py
+++ b/solution.py
@@ -70,7 +70,7 @@
             ]
         )
     ]
-    for load in loads:
+    for load in loads[:2]:
         load.start()
 
     barrier = pltpu.get_barrier_semaphore()
@@ -84,17 +84,15 @@
     def in_group(e):
         return ((e // 2) * 4 + zh * 2 + lax.rem(e, 2), h)
 
-    def greet_plane(d, carry):
-        greet((s, lax.rem(h + d, N)))
-        return carry
-
-    def greet_group(d, carry):
-        greet(in_group(lax.rem(pos + d, 8)))
-        return carry
-
-    lax.fori_loop(1, N, greet_plane, 0)
+    for d in (2, 1, 3, 0):
+        for z in (3 - zl, lax.rem(zl + 2, 4), zl + 1 - 2 * lax.rem(zl, 2), zl)[: 4 if d else 3]:
+            greet((s, lax.rem(x + d, 4) * 4 + z))
     greet(antipode)
-    lax.fori_loop(1, 8, greet_group, 0)
+    for e in far_first(y, c)[:7]:
+        greet(in_group(e))
+
+    for load in loads[2:]:
+        load.start()
 
     def copy(i, src, dst, device):
         return pltpu.make_async_remote_copy(
@@ -131,7 +129,8 @@
         copy(V_MOVE, v_hbm.at[:, part(j, HD)], values.at[slot], device).start()
         return carry
 
-    lax.fori_loop(1, YS, move_prompt, 0)
+    for d in (2, 1, 3):
+        move_prompt(d, 0)
 
     def move_w(d, carry):
         j = lax.rem(y + d, YS)
@@ -139,7 +138,8 @@
         copy(W_MOVE, wo_hbm.at[part(j, HD)], w_stage.at[part(y, HD)], device).start()
         return carry
 
-    lax.fori_loop(1, YS, move_w, 0)
+    for d in (2, 1, 3):
+        move_w(d, 0)
 
     mine_k = lax.rem(h, 2)
     mine = mine_k * 8 + h // 2
@@ -205,7 +205,8 @@
         copy(KV_RS, kv_far.at[part(j, 2 * HALF)], r_kv.at[part(y, 2 * HALF)], device).start()
         return carry
 
-    lax.fori_loop(1, YS, send_kv, 0)
+    for d in (2, 1, 3):
+        send_kv(d, 0)
     r_kv[part(y, 2 * HALF), :] = kv_far[part(y, 2 * HALF), :]
 
     q_sums = []
@@ -231,7 +232,8 @@
         copy(W_TURN, w_stage.at[part(i, HD)], w_all.at[part(x, HD)], (s, 4 * i + zl)).start()
         return carry
 
-    lax.fori_loop(1, 4, turn_w, 0)
+    for d in (2, 1, 3):
+        turn_w(d, 0)
     w_all[part(x, HD), :] = w_stage[part(x, HD), :]
 
     rows(KV_RS, r_kv, 6 * HALF).wait_recv()

time: 58.2 us -> 58.2 us (level)
  no operation moved by 1% of the time
where the time goes in v5:
time: 58.2 us; the launch traced here: 57.9 us
  Pallas kernels  56.6 us (97%)
  local copies, waits for them, and re-layouts  1.32 us (2%)
    pallas_call x1, Pallas kernels, body(): pl.pallas_call(kernel, out_shape=jax.ShapeDtypeStruct((B, F), bf16), in_s...  56.6 us
    unnamed x1, local copies, waits for them, and re-layouts  1.32 us

profile of v5, /device:TPU:64, one launch (start us, length us, event | category | flops | bytes accessed | tf_op | source)
XLA Modules:
  0.0 57.9 jit_solution(11560962124197277654)
XLA Ops:
  0.0 56.6 %shard_map.91 = bf16[16,512]{1,0:T(8,128)(2,1)} custom-call(s32[16,16]{1,0:T(8,128)} %ids_hbm.1, bf16[512,512]{1,0:T(8,128)(2,1)} %e_hbm.1, bf16[512,512]{1,0:T(8,128)(2,1)} %wq_hbm.1, bf16[512,512]{1,0:T(8,128)(2,1)} %wk_hbm.1, bf16[512,512]{1,0:T(8,128)(2,1)} %wv_hbm.1, bf16[512,512]{1,0:T(8,128)(2,1)} %wo_hbm.1, bf16[512,512]{1,0:T(8,128)(2,1)} %k_hbm.1, ...), custom_call_target="tpu_custom_call" | custom-call | tf_op jit(solution)/shard_map/pallas_call | solution.py:405
  56.6 1.3 %copy.11 = bf16[16,512]{1,0:T(8,128)(2,1)} copy(bf16[16,512]{1,0:T(8,128)(2,1)} %shard_map.91) | data formatting | bytes 32768
